TPU v7x, 32 devices: a whole 2x2x4 slice. The times are simulated.
32 devices in a mesh: fsdp: 32 (over z, y, x, core), tp: 1.
Axes of the slice: x: 2, y: 2, z: 4, core: 2. Of those that a mesh axis runs over, the one named last changes fastest.
Arguments:
- hidden_in: bfloat16 [32768, 5120], P('fsdp', 'tp'), may hold values from -6 to 6
- out_grad: bfloat16 [32768, 5120], P('fsdp', 'tp'), may hold values from -36 to 36
- rewards: float32 [64], P('fsdp'), may hold values from -5 to 5
- group_ids: int32 [64], replicated, may hold values from 0 to 7, as said below
- weight: bfloat16 [5120, 5120], P('fsdp', 'tp'), may hold values from -0.078125 to 0.078125
- adam_m: float32 [5120, 5120], P('fsdp', 'tp'), may hold values from -6 to 6
- adam_v: float32 [5120, 5120], P('fsdp', 'tp'), may hold values from 0.05 to 2
- given_queries: bfloat16 [512, 4, 5120], P('fsdp', None, 'tp'), may hold values from -24 to 24
- given_keys: bfloat16 [512, 4, 1024], P('fsdp', None, 'tp'), may hold values from -4 to 4
- given_values: bfloat16 [512, 4, 1024], P('fsdp', None, 'tp'), may hold values from -12 to 12
- stored_keys: bfloat16 [512, 8, 512, 128], P('fsdp', 'tp'), may hold values from -24 to 24
- stored_values: bfloat16 [512, 8, 512, 128], P('fsdp', 'tp'), may hold values from -12 to 12
- cache_fill_length: int32 [512], P('fsdp'), may hold values from 128 to 508
Outputs:
- new_weight: bfloat16 [5120, 5120], P('fsdp', 'tp')
- new_m: float32 [5120, 5120], P('fsdp', 'tp')
- new_v: float32 [5120, 5120], P('fsdp', 'tp')
- layer_out: float32 [512, 4, 5120], P('fsdp', None, 'tp')
Inputs may be any that keep to these rules, and one draw needn't show every extreme that they name: `group_ids`: each group number names exactly 8 sequences.
All inputs are finite; a program needn't handle non-finite values.
Results may differ from a plain program's by a relative error of at most 0.0059.
Values may be sent and summed in bfloat16 or wider, within the bound.
A program may use at most 384 MiB of HBM per device.

v0:
```python
import math

import jax
import jax.numpy as jnp
from jax import lax
from jax.sharding import PartitionSpec as P

GSIZE = 8
OPT_STEP = 10


beta_one = 0.9
beta_two = 0.95
adam_eps = 1e-08
learn_rate = 0.002
decay_rate = 0.1
std_floor = 0.75


def attend_local(query_in, key_new, value_new, key_cache, value_cache, lengths):
    row_count = query_in.shape[0]
    step_count = query_in.shape[1]
    kv_heads = key_cache.shape[1]
    cache_size = key_cache.shape[2]
    head_dim = key_cache.shape[3]
    group_size = query_in.shape[2] // (kv_heads * head_dim)
    scaling = 1.0 / math.sqrt(head_dim)
    query_heads = query_in.reshape(row_count, step_count, kv_heads, group_size, head_dim)
    fresh_keys = key_new.reshape(row_count, step_count, kv_heads, head_dim)
    fresh_values = value_new.reshape(row_count, step_count, kv_heads, head_dim)
    cache_score = (
        jnp.einsum("rsKgd,rKcd->rKgsc", query_heads, key_cache, preferred_element_type=jnp.float32)
        * scaling
    )
    fresh_score = (
        jnp.einsum("rsKgd,rtKd->rKgst", query_heads, fresh_keys, preferred_element_type=jnp.float32)
        * scaling
    )
    cache_mask = jnp.arange(cache_size, dtype=jnp.int32)[None, :] < lengths[:, None]
    step_index = jnp.arange(step_count, dtype=jnp.int32)
    fresh_mask = step_index[None, :] <= step_index[:, None]
    cache_score = jnp.where(cache_mask[:, None, None, None, :], cache_score, -jnp.inf)
    fresh_score = jnp.where(fresh_mask, fresh_score, -jnp.inf)
    peak_score = jnp.maximum(
        jnp.max(cache_score, axis=-1, keepdims=True), jnp.max(fresh_score, axis=-1, keepdims=True)
    )
    cache_exp = jnp.exp(cache_score - peak_score)
    fresh_exp = jnp.exp(fresh_score - peak_score)
    total_exp = jnp.sum(cache_exp, axis=-1, keepdims=True) + jnp.sum(
        fresh_exp, axis=-1, keepdims=True
    )
    cache_prob = (cache_exp / total_exp).astype(jnp.bfloat16)
    fresh_prob = (fresh_exp / total_exp).astype(jnp.bfloat16)
    mixed = jnp.einsum(
        "rKgsc,rKcd->rsKgd", cache_prob, value_cache, preferred_element_type=jnp.float32
    )
    mixed = mixed + jnp.einsum(
        "rKgst,rtKd->rsKgd", fresh_prob, fresh_values, preferred_element_type=jnp.float32
    )
    return mixed.reshape(row_count, step_count, kv_heads * group_size * head_dim).astype(
        jnp.bfloat16
    )


def per_device(
    hidden_in,
    out_grad,
    rewards,
    group_ids,
    weight,
    adam_m,
    adam_v,
    given_queries,
    given_keys,
    given_values,
    stored_keys,
    stored_values,
    cache_fill_length,
):
    seq_dev = rewards.shape[0]
    seq_total = seq_dev * lax.axis_size("fsdp")
    group_count = seq_total // GSIZE
    position = lax.axis_index("fsdp")
    local_ids = lax.dynamic_slice_in_dim(group_ids, position * seq_dev, seq_dev)
    labels = jnp.arange(group_count, dtype=jnp.int32)
    local_member = (local_ids[:, None] == labels[None, :]).astype(jnp.float32)
    every_reward = lax.all_gather(rewards, "fsdp", axis=0, tiled=True)
    member = (group_ids[:, None] == labels[None, :]).astype(jnp.float32)
    group_mean = jnp.sum(member * every_reward[:, None], axis=0) / GSIZE
    spread_all = every_reward - jnp.sum(member * group_mean[None, :], axis=1)
    group_var = jnp.sum(member * (spread_all * spread_all)[:, None], axis=0) / (GSIZE - 1)
    own_mean = jnp.sum(local_member * group_mean[None, :], axis=1)
    own_std = jnp.sqrt(jnp.sum(local_member * group_var[None, :], axis=1))
    advantage = (rewards - own_mean) / jnp.maximum(own_std, std_floor)
    token_count = hidden_in.shape[0]
    token_adv = jnp.repeat(advantage, token_count // seq_dev)
    weighted = (hidden_in.astype(jnp.float32) * token_adv[:, None] / seq_total).astype(jnp.bfloat16)
    full_grad = lax.all_gather(out_grad, "tp", axis=1, tiled=True)
    gradient = lax.psum_scatter(
        lax.dot_general(
            full_grad, weighted, (((0,), (0,)), ((), ())), preferred_element_type=jnp.float32
        ),
        "fsdp",
        scatter_dimension=0,
        tiled=True,
    )
    new_m = beta_one * adam_m + (1.0 - beta_one) * gradient
    new_v = beta_two * adam_v + (1.0 - beta_two) * gradient * gradient
    correct_one = 1.0 - beta_one**OPT_STEP
    correct_two = 1.0 - beta_two**OPT_STEP
    update = new_m / correct_one / (jnp.sqrt(new_v / correct_two) + adam_eps)
    new_weight = (
        weight.astype(jnp.float32) * (1.0 - learn_rate * decay_rate) - learn_rate * update
    ).astype(jnp.bfloat16)
    attn = attend_local(
        given_queries, given_keys, given_values, stored_keys, stored_values, cache_fill_length
    )
    row_count = attn.shape[0]
    step_count = attn.shape[1]
    attn_flat = attn.reshape(row_count * step_count, attn.shape[2])
    partial_out = lax.dot_general(
        attn_flat,
        lax.all_gather(new_weight, "fsdp", axis=0, tiled=True),
        (((1,), (1,)), ((), ())),
        preferred_element_type=jnp.float32,
    )
    summed = lax.psum_scatter(partial_out, "tp", scatter_dimension=1, tiled=True)
    layer_out = summed.reshape(row_count, step_count, summed.shape[1])
    return (new_weight, new_m, new_v, layer_out)


def solution(mesh):
    in_specs = (
        P("fsdp", "tp"),
        P("fsdp", "tp"),
        P("fsdp"),
        P(),
        P("fsdp", "tp"),
        P("fsdp", "tp"),
        P("fsdp", "tp"),
        P("fsdp", None, "tp"),
        P("fsdp", None, "tp"),
        P("fsdp", None, "tp"),
        P("fsdp", "tp", None, None),
        P("fsdp", "tp", None, None),
        P("fsdp"),
    )
    out_specs = (P("fsdp", "tp"), P("fsdp", "tp"), P("fsdp", "tp"), P("fsdp", None, "tp"))
    return jax.shard_map(
        per_device, mesh=mesh, in_specs=in_specs, out_specs=out_specs, check_vma=False
    )
```

profile of v0, /device:TPU:0, one launch (start us, length us, event | category | flops | bytes accessed | tf_op | source)
XLA Modules:
  0.0 1650.2 jit_solution(8128850846004554187)
XLA Ops:
  7.2 0.0 copy-start
  7.2 0.0 reduce-scatter.4.cloned.1.call-start
  7.2 0.9 dynamic-update-slice
  8.1 42.0 %all-reduce = f32[64]{0:T(128)S(1)} all-reduce(f32[64]{0:T(128)S(1)} %dynamic-update-slice), channel_id=1, replica_groups=mesh['fsdp'=32,'tp'=1] {'fsdp'}, use_global_device_ids=true, to_apply=%add | all-reduce | flops 64 | bytes 512
  50.1 0.8 select_reduce_fusion.2
  50.9 0.7 dynamic_slice.3
  51.6 0.7 select_reduce_fusion.1
  52.3 0.8 select_reduce_fusion
  53.1 0.2 select_reduce_fusion.4
  53.3 0.7 maximum_divide_fusion
  54.0 0.1 broadcast_bitcast_fusion
  54.0 66.3 %convolution_bitcast_fusion = f32[5120,5120]{0,1:T(8,128)} fusion(bf16[1024,5120]{1,0:T(8,128)(2,1)} %param.14, bf16[1024,5120]{1,0:T(8,128)(2,1)} %param.13, f32[1024]{0:T(1024)S(1)} %bitcast.59), kind=kOutput, calls=%fused_computation | convolution fusion | flops 53708062720 | bytes 125833216 | tf_op jit(solution)/shard_map/dot_general | solution.py:100
  120.3 104.0 %copy.85 = f32[5120,5120]{1,0:T(8,128)} copy(f32[5120,5120]{0,1:T(8,128)} %convolution_bitcast_fusion) | data formatting | bytes 209715200
  224.3 0.0 copy-start.2
  224.3 0.0 reduce-scatter.4.cloned.1.call-update
  224.3 0.0 copy-start.3
  224.3 0.0 copy-start.4
  224.3 0.2 all-gather.2.cloned.1.call-start
  224.6 1093.6 %reduce-scatter.4.cloned.1.call-done = f32[160,5120]{1,0:T(8,128)} async-done(((f32[5120,5120]{1,0:T(8,128)}), f32[160,5120]{1,0:T(8,128)}) %reduce-scatter.4.cloned.1.call-update) | async-done | bytes 3276816 | tf_op jit(solution)/shard_map/reduce_scatter | solution.py:99
  1318.1 0.0 copy-done.2
  1318.1 6.3 subtract_convert_fusion
  1324.4 0.0 all-gather.2.cloned.1.call-update
  1324.4 1.9 reshape.76
  1326.4 0.0 copy-done.3
  1326.4 0.1 iota_compare_fusion
  1326.5 0.0 copy-done.4
  1326.5 4.7 fusion.30
  1331.2 11.4 bitcast_reduce_fusion
  1342.6 0.0 copy-start.1
  1342.6 0.1 max.12
  1342.7 1.0 fusion.21
  1343.7 6.6 fusion.9
  1350.3 0.1 add.35
  1350.4 0.0 copy-done.1
  1350.4 8.4 fusion.2
  1358.8 0.0 copy-done
  1358.8 0.8 fusion.16
  1359.6 0.3 copy.79
  1359.9 0.7 convert_element_type.39
  1360.6 259.0 %all-gather.2.cloned.1.call-done = bf16[5120,5120]{1,0:T(8,128)(2,1)} async-done(((bf16[160,5120]{1,0:T(8,128)(2,1)}), bf16[5120,5120]{1,0:T(8,128)(2,1)}) %all-gather.2.cloned.1.call-update) | async-done | bytes 52428816 | tf_op jit(solution)/shard_map/all_gather | solution.py:123
  1619.6 21.8 %fusion = f32[16,4,5120]{2,0,1:T(8,128)S(1)} fusion(bf16[16,4,5120]{2,0,1:T(8,128)(2,1)S(1)} %convert_element_type.39, bf16[5120,5120]{1,0:T(8,128)(2,1)} %all-gather.2.cloned.1.call-done), kind=kOutput, calls=%fused_computation.1 | convolution fusion | flops 3355443200 | bytes 54394880 | tf_op jit(solution)/shard_map/dot_general | solution.py:121
  1641.4 1.9 copy.80
  (6 shorter events, 0.0 us)
Async XLA Ops:
  7.2 1351.6 %copy-start = (bf16[16,4,1024]{2,1,0:T(4,128)(2,1)S(1)}, bf16[16,4,1024]{2,1,0:T(4,128)(2,1)}, u32[]{:S(2)}) copy-start(bf16[16,4,1024]{2,1,0:T(4,128)(2,1)} %param.22) | copy-start | bytes 393220
  7.2 1310.9 %reduce-scatter.4.cloned.1.call-start = ((), (), s32[]{:S(2)}) async-start(), calls=%async_computation.2 | async-start | bytes 108134400 | tf_op jit(solution)/shard_map/reduce_scatter | solution.py:99
  224.3 1093.8 %copy-start.2 = (f32[160,5120]{1,0:T(8,128)S(1)}, f32[160,5120]{1,0:T(8,128)}, u32[]{:S(2)}) copy-start(f32[160,5120]{1,0:T(8,128)} %param.18) | copy-start | bytes 9830404
  224.3 1102.1 %copy-start.3 = (s32[16]{0:T(128)S(1)}, s32[16]{0:T(128)}, u32[]{:S(2)}) copy-start(s32[16]{0:T(128)} %param.25) | copy-start | bytes 196
  224.3 1102.2 %copy-start.4 = (bf16[16,4,1024]{2,1,0:T(4,128)(2,1)S(1)}, bf16[16,4,1024]{2,1,0:T(4,128)(2,1)}, u32[]{:S(2)}) copy-start(bf16[16,4,1024]{2,1,0:T(4,128)(2,1)} %param.21) | copy-start | bytes 393220
  224.3 1395.3 %all-gather.2.cloned.1.call-start = ((), (), s32[]{:S(2)}) async-start(), calls=%async_computation.1 | async-start | bytes 54067200 | tf_op jit(solution)/shard_map/all_gather | solution.py:123
  1342.6 7.7 copy-start.1
Sparse Core Ops, SparseCore 0:
  224.4 1093.6 reduce-scatter.3
  1324.6 294.9 all-gather.1
where the time goes:
time: 1650 us
  waiting for transfers between devices  1350 us (82%)
  matrix products  113 us (7%)
  local copies, waits for them, and re-layouts  111 us (7%)
  blocking collectives  42 us (3%)
  other arithmetic  17.2 us (1%)
    reduce_scatter x1, waiting for transfers between devices, per_device(): lax.psum_scatter(lax.dot_general(full_grad, weighted, (((0,), (0,)), ((),...  1090 us
    all_gather x1, waiting for transfers between devices, per_device(): lax.all_gather(new_weight, 'fsdp', axis=0, tiled=True)  259 us
    unnamed x16, local copies, waits for them, and re-layouts  107 us
    dot_general x1, matrix products, per_device(): lax.dot_general(full_grad, weighted, (((0,), (0,)), ((), ())), preferred_...  66.3 us
    unnamed x1, blocking collectives  42 us
  transfers between devices with their start and end apart: 2, of which 2 were waited for; matrix products, arithmetic and copies ran while one was open for 2% of the time, Pallas kernels for 0%

commit v1 on v0

--- a/solution.py
+++ b/solution.py
@@ -59,6 +59,86 @@
     )
     return mixed.reshape(row_count, step_count, kv_heads * group_size * head_dim).astype(
         jnp.bfloat16
+    )
+
+
+def bit_swap(axis_total, bit):
+    return [(i, i ^ bit) for i in range(axis_total)]
+
+
+def depth_shift(axis_total, step):
+    return [(i, (i + 8 * step) % axis_total) for i in range(axis_total)]
+
+
+def take_half(blocks, which, axis):
+    return lax.dynamic_index_in_dim(blocks, which, axis, keepdims=False)
+
+
+def add_halves(kept, received):
+    return (kept.astype(jnp.float32) + received.astype(jnp.float32)).astype(jnp.bfloat16)
+
+
+def pick(blocks, which, axis):
+    low = lax.index_in_dim(blocks, 0, axis, keepdims=False)
+    high = lax.index_in_dim(blocks, 1, axis, keepdims=False)
+    return jnp.where(which == 0, low, high)
+
+
+def exchange_half(blocks, mine, axis, perm):
+    received = lax.ppermute(pick(blocks, 1 - mine, axis), "fsdp", perm)
+    return add_halves(pick(blocks, mine, axis), received)
+
+
+def column_pieces(width, count):
+    tiles = width // 128
+    if width % 128 or tiles < count:
+        return [(0, width)]
+    edges = [128 * (tiles * i // count) for i in range(count + 1)]
+    return [(edges[i], edges[i + 1]) for i in range(count)]
+
+
+def summed_rows(pair_grad, pair_weighted, position, axis_total):
+    depth = axis_total // 8
+    my_z = position // 8
+    my_y = (position // 4) % 2
+    my_x = (position // 2) % 2
+    my_core = position % 2
+    row_total = pair_grad.shape[1]
+    rows_chip = row_total // (axis_total // 2)
+    finished = []
+    for low, high in column_pieces(pair_weighted.shape[1], 5):
+        partial = lax.dot_general(
+            pair_grad,
+            pair_weighted[:, low:high],
+            (((0,), (0,)), ((), ())),
+            preferred_element_type=jnp.float32,
+        ).astype(jnp.bfloat16)
+        width = high - low
+        blocks = partial.reshape(depth, 2, 2, rows_chip, width)
+        first = blocks[..., : width // 2]
+        second = blocks[..., width // 2 :]
+        first = exchange_half(first, my_x, 2, bit_swap(axis_total, 2))
+        second = exchange_half(second, my_y, 1, bit_swap(axis_total, 4))
+        first = exchange_half(first, my_y, 1, bit_swap(axis_total, 4))
+        second = exchange_half(second, my_x, 1, bit_swap(axis_total, 2))
+        both = jnp.concatenate([first, second], axis=-1)
+        total = take_half(both, my_z, 0).astype(jnp.float32)
+        for step in range(1, depth):
+            outgoing = take_half(both, lax.rem(my_z + step, depth), 0)
+            arrived = lax.ppermute(outgoing, "fsdp", depth_shift(axis_total, step))
+            total = total + arrived.astype(jnp.float32)
+        finished.append(total)
+    chip_rows = jnp.concatenate(finished, axis=1)
+    own_rows = chip_rows.shape[0] // 2
+    halves = chip_rows.reshape(2, own_rows, chip_rows.shape[1])
+    mine = take_half(halves, my_core, 0)
+    theirs = lax.ppermute(
+        take_half(halves, 1 - my_core, 0), "fsdp", bit_swap(axis_total, 1)
+    )
+    return jnp.where(
+        my_core == 0,
+        jnp.concatenate([mine, theirs], axis=1),
+        jnp.concatenate([theirs, mine], axis=1),
     )
 
 
@@ -81,29 +161,33 @@
     seq_total = seq_dev * lax.axis_size("fsdp")
     group_count = seq_total // GSIZE
     position = lax.axis_index("fsdp")
-    local_ids = lax.dynamic_slice_in_dim(group_ids, position * seq_dev, seq_dev)
     labels = jnp.arange(group_count, dtype=jnp.int32)
-    local_member = (local_ids[:, None] == labels[None, :]).astype(jnp.float32)
     every_reward = lax.all_gather(rewards, "fsdp", axis=0, tiled=True)
     member = (group_ids[:, None] == labels[None, :]).astype(jnp.float32)
     group_mean = jnp.sum(member * every_reward[:, None], axis=0) / GSIZE
     spread_all = every_reward - jnp.sum(member * group_mean[None, :], axis=1)
     group_var = jnp.sum(member * (spread_all * spread_all)[:, None], axis=0) / (GSIZE - 1)
-    own_mean = jnp.sum(local_member * group_mean[None, :], axis=1)
-    own_std = jnp.sqrt(jnp.sum(local_member * group_var[None, :], axis=1))
-    advantage = (rewards - own_mean) / jnp.maximum(own_std, std_floor)
+    group_std = jnp.sqrt(group_var)
+    own_std = jnp.sum(member * group_std[None, :], axis=1)
+    advantage = spread_all / jnp.maximum(own_std, std_floor)
+    axis_total = lax.axis_size("fsdp")
+    core = position % 2
+    swap_core = bit_swap(axis_total, 1)
     token_count = hidden_in.shape[0]
-    token_adv = jnp.repeat(advantage, token_count // seq_dev)
-    weighted = (hidden_in.astype(jnp.float32) * token_adv[:, None] / seq_total).astype(jnp.bfloat16)
     full_grad = lax.all_gather(out_grad, "tp", axis=1, tiled=True)
-    gradient = lax.psum_scatter(
-        lax.dot_general(
-            full_grad, weighted, (((0,), (0,)), ((), ())), preferred_element_type=jnp.float32
-        ),
-        "fsdp",
-        scatter_dimension=0,
-        tiled=True,
-    )
+    half_width = hidden_in.shape[1] // 2
+    low_half, high_half = hidden_in[:, :half_width], hidden_in[:, half_width:]
+    other_grad = lax.ppermute(full_grad, "fsdp", swap_core)
+    other_hidden = lax.ppermute(jnp.where(core == 0, high_half, low_half), "fsdp", swap_core)
+    pair_grad = jnp.concatenate([full_grad, other_grad], axis=0)
+    pair_hidden = jnp.concatenate([jnp.where(core == 0, low_half, high_half), other_hidden], axis=0)
+    own_adv = lax.dynamic_slice_in_dim(advantage, position * seq_dev, seq_dev)
+    other_adv = lax.dynamic_slice_in_dim(advantage, (position + 1 - 2 * core) * seq_dev, seq_dev)
+    pair_adv = jnp.repeat(jnp.concatenate([own_adv, other_adv]), token_count // seq_dev)
+    pair_weighted = (
+        pair_hidden.astype(jnp.float32) * pair_adv[:, None] / seq_total
+    ).astype(jnp.bfloat16)
+    gradient = summed_rows(pair_grad, pair_weighted, position, axis_total)
     new_m = beta_one * adam_m + (1.0 - beta_one) * gradient
     new_v = beta_two * adam_v + (1.0 - beta_two) * gradient * gradient
     correct_one = 1.0 - beta_one**OPT_STEP
@@ -118,12 +202,13 @@
     row_count = attn.shape[0]
     step_count = attn.shape[1]
     attn_flat = attn.reshape(row_count * step_count, attn.shape[2])
-    partial_out = lax.dot_general(
-        attn_flat,
-        lax.all_gather(new_weight, "fsdp", axis=0, tiled=True),
-        (((1,), (1,)), ((), ())),
-        preferred_element_type=jnp.float32,
-    )
+    every_attn = lax.all_gather(attn_flat, "fsdp", axis=0, tiled=True)
+    own_features = lax.dot_general(
+        every_attn, new_weight, (((1,), (1,)), ((), ())), preferred_element_type=jnp.float32
+    ).astype(jnp.bfloat16)
+    partial_out = lax.all_to_all(
+        own_features, "fsdp", split_axis=0, concat_axis=1, tiled=True
+    ).astype(jnp.float32)
     summed = lax.psum_scatter(partial_out, "tp", scatter_dimension=1, tiled=True)
     layer_out = summed.reshape(row_count, step_count, summed.shape[1])
     return (new_weight, new_m, new_v, layer_out)

time: 1650 us -> 583 us (0.35)
  waiting for transfers between devices: 1350 us -> 189 us
  starting transfers between devices: 0.26 us -> 78.3 us
  local copies, waits for them, and re-layouts: 111 us -> 39.6 us
  other arithmetic: 17.2 us -> 56.8 us
  blocking collectives: 42 us -> 74.8 us
    reduce_scatter x1 -> x0, waiting for transfers between devices: 1090 us -> none  [per_device(): lax.psum_scatter(lax.dot_general(full_grad, weighted, (((0,), (0,)), ((),...]
    all_gather x1, waiting for transfers between devices: 259 us -> 0.01 us  [per_device(): every_attn = lax.all_gather(attn_flat, 'fsdp', axis=0, tiled=True)]
    ppermute x0 -> x38, waiting for transfers between devices: none -> 189 us  [the longest x20 118 us: exchange_half(): received = lax.ppermute(pick(blocks, 1 - mine, axis), 'fsdp', perm)]
    unnamed x16 -> x41, local copies, waits for them, and re-layouts: 107 us -> 13.8 us
    ppermute x0 -> x38, starting transfers between devices: none -> 78.2 us  [the longest x15 57.9 us: summed_rows(): arrived = lax.ppermute(outgoing, 'fsdp', depth_shift(axis_total, step))]
    all_to_all x0 -> x1, blocking collectives: none -> 30.2 us  [per_device(): lax.all_to_all(own_features, 'fsdp', split_axis=0, concat_axis=1, tiled=T...]
    convert_element_type x0 -> x22, other arithmetic: none -> 26 us  [the longest x20 14.9 us: add_halves(): (kept.astype(jnp.float32) + received.astype(jnp.float32)).astype(jnp.bflo...]
    select_n x0 -> x21, other arithmetic: none -> 17.4 us  [the longest x1 8.91 us: per_device(): jnp.where(core == 0, low_half, high_half)]
  transfers between devices with their start and end apart: 2 -> 39, of which waited for: 2 -> 16; matrix products, arithmetic and copies ran while one was open for 2% -> 34% of each run, Pallas kernels for 0% -> 0%
where the time goes in v1:
time: 583 us; the launch traced here: 575 us
  waiting for transfers between devices  189 us (32%)
  matrix products  122 us (21%)
  starting transfers between devices  78.3 us (13%)
  blocking collectives  74.8 us (13%)
  other arithmetic  56.8 us (10%)
  local copies, waits for them, and re-layouts  39.6 us (7%)
  between operations  15.2 us (3%)
    ppermute x20, waiting for transfers between devices, exchange_half(): received = lax.ppermute(pick(blocks, 1 - mine, axis), 'fsdp', perm)  118 us
    dot_general x5, matrix products, summed_rows(): lax.dot_general(pair_grad, pair_weighted[:, low:high], (((0,), (0,)), (()...  85.3 us
    ppermute x15, waiting for transfers between devices, summed_rows(): arrived = lax.ppermute(outgoing, 'fsdp', depth_shift(axis_total, step))  67 us
    ppermute x15, starting transfers between devices, summed_rows(): arrived = lax.ppermute(outgoing, 'fsdp', depth_shift(axis_total, step))  57.9 us
    unnamed x1, blocking collectives  44.6 us
    all_to_all x1, blocking collectives, per_device(): lax.all_to_all(own_features, 'fsdp', split_axis=0, concat_axis=1, tiled=T...  30.2 us
    ppermute x20, starting transfers between devices, exchange_half(): received = lax.ppermute(pick(blocks, 1 - mine, axis), 'fsdp', perm)  19.7 us
    convert_element_type x20, other arithmetic, add_halves(): (kept.astype(jnp.float32) + received.astype(jnp.float32)).astype(jnp.bflo...  14.9 us
  transfers between devices with their start and end apart: 39, of which 16 were waited for; matrix products, arithmetic and copies ran while one was open for 34% of the time, Pallas kernels for 0%

profile of v1, /device:TPU:0, one launch (start us, length us, event | category | flops | bytes accessed | tf_op | source)
XLA Modules:
  0.0 575.0 jit_solution(10153678066411951415)
XLA Ops:
  8.5 1.9 reshape.257
  10.4 11.2 %bitcast_reduce_fusion = (f32[16,8,5,4]{2,3,1,0:T(4,128)S(1)}, f32[16,8,512,4,5]{2,4,3,1,0:T(8,128)}) fusion(pred[16,512]{1,0:T(8,128)(4,1)S(1)} %iota_compare_fusion, bf16[16,4,8,5,128]{4,3,2,1,0:T(8,128)(2,1)S(1)} %reshape.257, bf16[16,8,512,128]{3,2,1,0:T(8,128)(2,1)} %param.23), kind=kOutput, calls=%fused_computation.6 | convolution fusion | flops 339473920 | bytes 22693888 | tf_op jit(solution)/shard_map/rsKgd,rKcd->rKgsc/dot_general | solution.py:32
  21.7 4.7 fusion.120
  26.5 5.5 fusion.5
  33.1 8.3 %fusion = f32[16,8,5,4,128]{4,2,3,1,0:T(8,128)S(1)} fusion(bf16[16,8,512,128]{3,2,1,0:T(8,128)(2,1)} %param.24, f32[16,8,512,4,5]{2,4,3,1,0:T(8,128)S(1)} %bitcast.242, f32[16,8,5,4]{2,3,1,0:T(4,128)S(1)} %add.265, f32[16,8,5,4]{2,3,1,0:T(4,128)S(1)} %max.16, pred[16,512]{1,0:T(8,128)(4,1)S(1)} %iota_compare_fusion), kind=kOutput, calls=%fused_computation.1 | convolution fusion | flops 342097920 | bytes 23359488 | tf_op jit(solution)/shard_map/rKgsc,rKcd->rsKgd/dot_general | solution.py:54
  44.2 8.9 %broadcast_select_fusion.1 = (bf16[1024,2560]{1,0:T(8,128)(2,1)}, bf16[1024,2560]{1,0:T(8,128)(2,1)}) fusion(pred[]{:T(512)S(6)} %eq.21, bf16[1024,5120]{1,0:T(8,128)(2,1)} %param.13), kind=kLoop, calls=%fused_computation.17 | loop fusion | flops 5242880 | bytes 20971520 | tf_op jit(solution)/shard_map/jit(_where)/select_n | solution.py:183
  53.3 44.6 %all-reduce = f32[64]{0:T(128)S(1)} all-reduce(f32[64]{0:T(128)S(1)} %dynamic-update-slice), channel_id=1, replica_groups=mesh['fsdp'=32,'tp'=1] {'fsdp'}, use_global_device_ids=true, to_apply=%add | all-reduce | flops 64 | bytes 512
  98.6 8.8 %constant_dynamic-update-slice_fusion.1 = bf16[2048,5120]{1,0:T(8,128)(2,1)} fusion(bf16[1024,5120]{1,0:T(8,128)(2,1)} %param.14), kind=kLoop, calls=%fused_computation.219 | loop fusion | bytes 20971520
  107.4 10.9 %multiply_convert_fusion = bf16[2048,2560]{1,0:T(8,128)(2,1)} fusion(bf16[1024,2560]{1,0:T(8,128)(2,1)} %collective-permute-done.1, bf16[1024,2560]{1,0:T(8,128)(2,1)} %get-tuple-element.9, f32[2048]{0:T(1024)S(1)} %bitcast.255), kind=kLoop, calls=%fused_computation | loop fusion | flops 36700160 | bytes 20979712 | tf_op jit(solution)/shard_map/convert_element_type | solution.py:189
  118.3 10.0 %constant_dynamic-update-slice_fusion = bf16[2048,5120]{1,0:T(8,128)(2,1)} fusion(bf16[2048,5120]{1,0:T(8,128)(2,1)} %constant_dynamic-update-slice_fusion.1, bf16[1024,5120]{1,0:T(8,128)(2,1)} %collective-permute-done), kind=kLoop, calls=%fused_computation.218 | loop fusion | bytes 20971520 | tf_op jit(solution)/shard_map/concatenate | solution.py:182
  128.3 16.0 %convolution_convert_fusion.4 = bf16[5120,512]{1,0:T(8,128)(2,1)S(1)} fusion(bf16[2048,5120]{1,0:T(8,128)(2,1)} %constant_dynamic-update-slice_fusion, bf16[2048,2560]{1,0:T(8,128)(2,1)} %multiply_convert_fusion), kind=kOutput, calls=%fused_computation.14 | convolution fusion | flops 10740039680 | bytes 28311552 | tf_op jit(solution)/shard_map/dot_general | solution.py:110
  147.9 2.1 select_bitcast_fusion.8
  151.4 16.3 %convolution_convert_fusion.3 = bf16[5120,512]{1,0:T(8,128)(2,1)S(1)} fusion(bf16[2048,5120]{1,0:T(8,128)(2,1)} %constant_dynamic-update-slice_fusion, bf16[2048,2560]{1,0:T(8,128)(2,1)} %multiply_convert_fusion), kind=kOutput, calls=%fused_computation.13 | convolution fusion | flops 10740039680 | bytes 28311552 | tf_op jit(solution)/shard_map/dot_general | solution.py:110
  171.3 17.7 %convolution_convert_fusion.2 = bf16[5120,512]{1,0:T(8,128)(2,1)} fusion(bf16[2048,5120]{1,0:T(8,128)(2,1)} %constant_dynamic-update-slice_fusion, bf16[2048,2560]{1,0:T(8,128)(2,1)} %multiply_convert_fusion), kind=kOutput, calls=%fused_computation.12 | convolution fusion | flops 10740039680 | bytes 28311552 | tf_op jit(solution)/shard_map/dot_general | solution.py:110
  189.0 2.1 fusion.115
  194.4 17.7 %convolution_convert_fusion.1 = bf16[5120,512]{1,0:T(8,128)(2,1)} fusion(bf16[2048,5120]{1,0:T(8,128)(2,1)} %constant_dynamic-update-slice_fusion, bf16[2048,2560]{1,0:T(8,128)(2,1)} %multiply_convert_fusion), kind=kOutput, calls=%fused_computation.11 | convolution fusion | flops 10740039680 | bytes 28311552 | tf_op jit(solution)/shard_map/dot_general | solution.py:110
  212.1 2.1 fusion.113
  215.6 17.6 %convolution_convert_fusion = bf16[5120,512]{1,0:T(8,128)(2,1)} fusion(bf16[2048,5120]{1,0:T(8,128)(2,1)} %constant_dynamic-update-slice_fusion, bf16[2048,2560]{1,0:T(8,128)(2,1)} %multiply_convert_fusion), kind=kOutput, calls=%fused_computation.10 | convolution fusion | flops 10740039680 | bytes 28311552 | tf_op jit(solution)/shard_map/dot_general | solution.py:110
  233.2 2.1 fusion.111
  239.0 2.0 fusion.20
  242.3 1.9 fusion.21
  245.4 1.9 fusion.19
  248.2 1.9 fusion.18
  251.1 1.9 fusion.17
  253.1 16.2 %collective-permute-done.18 = bf16[4,2,320,256]{3,2,0,1:T(8,128)(2,1)S(1)} collective-permute-done((bf16[4,2,320,256]{3,2,0,1:T(8,128)(2,1)S(1)}, bf16[4,2,320,256]{3,2,0,1:T(8,128)(2,1)S(1)}, u32[]{:S(2)}, u32[]{:S(2)}) %collective-permute-start.18) | collective-permute-done | bytes 1310752 | tf_op jit(solution)/shard_map/ppermute | solution.py:88
  273.8 23.5 %collective-permute-done.25 = bf16[4,2,320,256]{3,2,0,1:T(8,128)(2,1)S(1)} collective-permute-done((bf16[4,2,320,256]{3,2,0,1:T(8,128)(2,1)S(1)}, bf16[4,2,320,256]{3,2,0,1:T(8,128)(2,1)S(1)}, u32[]{:S(2)}, u32[]{:S(2)}) %collective-permute-start.25) | collective-permute-done | bytes 1310752 | tf_op jit(solution)/shard_map/ppermute | solution.py:88
  301.8 23.6 %collective-permute-done.32 = bf16[4,2,320,256]{3,2,0,1:T(8,128)(2,1)S(1)} collective-permute-done((bf16[4,2,320,256]{3,2,0,1:T(8,128)(2,1)S(1)}, bf16[4,2,320,256]{3,2,0,1:T(8,128)(2,1)S(1)}, u32[]{:S(2)}, u32[]{:S(2)}) %collective-permute-start.32) | collective-permute-done | bytes 1310752 | tf_op jit(solution)/shard_map/ppermute | solution.py:88
  327.7 11.8 %collective-permute-done.3 = bf16[4,320,256]{2,1,0:T(8,128)(2,1)S(1)} collective-permute-done((bf16[4,320,256]{2,1,0:T(8,128)(2,1)S(1)}, bf16[4,320,256]{2,1,0:T(8,128)(2,1)S(1)}, u32[]{:S(2)}, u32[]{:S(2)}) %collective-permute-start.3) | collective-permute-done | bytes 655392 | tf_op jit(solution)/shard_map/ppermute | solution.py:88
  341.8 11.7 %collective-permute-done.10 = bf16[4,320,256]{2,1,0:T(8,128)(2,1)S(1)} collective-permute-done((bf16[4,320,256]{2,1,0:T(8,128)(2,1)S(1)}, bf16[4,320,256]{2,1,0:T(8,128)(2,1)S(1)}, u32[]{:S(2)}, u32[]{:S(2)}) %collective-permute-start.10) | collective-permute-done | bytes 655392 | tf_op jit(solution)/shard_map/ppermute | solution.py:88
  356.0 11.6 %collective-permute-done.17 = bf16[4,320,256]{2,1,0:T(8,128)(2,1)S(1)} collective-permute-done((bf16[4,320,256]{2,1,0:T(8,128)(2,1)S(1)}, bf16[4,320,256]{2,1,0:T(8,128)(2,1)S(1)}, u32[]{:S(2)}, u32[]{:S(2)}) %collective-permute-start.17) | collective-permute-done | bytes 655392 | tf_op jit(solution)/shard_map/ppermute | solution.py:88
  368.1 3.0 collective-permute-start.8
  371.4 10.2 %collective-permute-done.24 = bf16[4,320,256]{2,1,0:T(8,128)(2,1)S(1)} collective-permute-done((bf16[4,320,256]{2,1,0:T(8,128)(2,1)S(1)}, bf16[4,320,256]{2,1,0:T(8,128)(2,1)S(1)}, u32[]{:S(2)}, u32[]{:S(2)}) %collective-permute-start.24) | collective-permute-done | bytes 655392 | tf_op jit(solution)/shard_map/ppermute | solution.py:88
  381.6 2.2 collective-permute-start.7
  385.8 6.5 %collective-permute-done.31 = bf16[4,320,256]{2,1,0:T(8,128)(2,1)S(1)} collective-permute-done((bf16[4,320,256]{2,1,0:T(8,128)(2,1)S(1)}, bf16[4,320,256]{2,1,0:T(8,128)(2,1)S(1)}, u32[]{:S(2)}, u32[]{:S(2)}) %collective-permute-start.31) | collective-permute-done | bytes 655392 | tf_op jit(solution)/shard_map/ppermute | solution.py:88
  392.4 2.9 collective-permute-start.15
  397.4 15.3 %collective-permute-done.7 = bf16[320,512]{1,0:T(8,128)(2,1)S(1)} collective-permute-done((bf16[320,512]{1,0:T(8,128)(2,1)S(1)}, bf16[320,512]{1,0:T(8,128)(2,1)S(1)}, u32[]{:S(2)}, u32[]{:S(2)}) %collective-permute-start.7) | collective-permute-done | bytes 327712 | tf_op jit(solution)/shard_map/ppermute | solution.py:128
  412.8 17.6 %collective-permute-start.21 = (bf16[320,512]{1,0:T(8,128)(2,1)S(1)}, bf16[320,512]{1,0:T(8,128)(2,1)S(1)}, u32[]{:S(2)}, u32[]{:S(2)}) collective-permute-start(bf16[320,512]{1,0:T(8,128)(2,1)S(1)} %get-tuple-element.41), channel_id=1, source_target_pairs={{0,16},{1,17},{2,18},{3,19},{4,20},{5,21},{6,22},{7,23},{8,24},{9,... | collective-permute-start | bytes 983048 | tf_op jit(solution)/shard_map/ppermute | solution.py:128
  430.4 13.3 %collective-permute-done.14 = bf16[320,512]{1,0:T(8,128)(2,1)S(1)} collective-permute-done((bf16[320,512]{1,0:T(8,128)(2,1)S(1)}, bf16[320,512]{1,0:T(8,128)(2,1)S(1)}, u32[]{:S(2)}, u32[]{:S(2)}) %collective-permute-start.14) | collective-permute-done | bytes 327712 | tf_op jit(solution)/shard_map/ppermute | solution.py:128
  443.9 14.6 %collective-permute-start.28 = (bf16[320,512]{1,0:T(8,128)(2,1)S(1)}, bf16[320,512]{1,0:T(8,128)(2,1)S(1)}, u32[]{:S(2)}, u32[]{:S(2)}) collective-permute-start(bf16[320,512]{1,0:T(8,128)(2,1)S(1)} %get-tuple-element.38), channel_id=1, source_target_pairs={{0,16},{1,17},{2,18},{3,19},{4,20},{5,21},{6,22},{7,23},{8,24},{9,... | collective-permute-start | bytes 983048 | tf_op jit(solution)/shard_map/ppermute | solution.py:128
  458.6 13.1 %collective-permute-done.21 = bf16[320,512]{1,0:T(8,128)(2,1)S(1)} collective-permute-done((bf16[320,512]{1,0:T(8,128)(2,1)S(1)}, bf16[320,512]{1,0:T(8,128)(2,1)S(1)}, u32[]{:S(2)}, u32[]{:S(2)}) %collective-permute-start.21) | collective-permute-done | bytes 327712 | tf_op jit(solution)/shard_map/ppermute | solution.py:128
  471.8 14.8 %collective-permute-start.35 = (bf16[320,512]{1,0:T(8,128)(2,1)S(1)}, bf16[320,512]{1,0:T(8,128)(2,1)S(1)}, u32[]{:S(2)}, u32[]{:S(2)}) collective-permute-start(bf16[320,512]{1,0:T(8,128)(2,1)S(1)} %get-tuple-element.35), channel_id=1, source_target_pairs={{0,16},{1,17},{2,18},{3,19},{4,20},{5,21},{6,22},{7,23},{8,24},{9,... | collective-permute-start | bytes 983048 | tf_op jit(solution)/shard_map/ppermute | solution.py:128
  486.7 13.1 %collective-permute-done.28 = bf16[320,512]{1,0:T(8,128)(2,1)S(1)} collective-permute-done((bf16[320,512]{1,0:T(8,128)(2,1)S(1)}, bf16[320,512]{1,0:T(8,128)(2,1)S(1)}, u32[]{:S(2)}, u32[]{:S(2)}) %collective-permute-start.28) | collective-permute-done | bytes 327712 | tf_op jit(solution)/shard_map/ppermute | solution.py:128
  500.0 12.1 %collective-permute-done.35 = bf16[320,512]{1,0:T(8,128)(2,1)S(1)} collective-permute-done((bf16[320,512]{1,0:T(8,128)(2,1)S(1)}, bf16[320,512]{1,0:T(8,128)(2,1)S(1)}, u32[]{:S(2)}, u32[]{:S(2)}) %collective-permute-start.35) | collective-permute-done | bytes 327712 | tf_op jit(solution)/shard_map/ppermute | solution.py:128
  512.7 3.5 collective-permute-done.37
  516.2 4.3 subtract_convert_fusion
  521.7 11.2 %convolution_convert_fusion.5 = bf16[2048,160]{0,1:T(8,128)(2,1)S(1)} fusion(bf16[2048,5120]{1,0:T(8,128)(2,1)} %all-gather.2.cloned.1.call-done, bf16[160,5120]{1,0:T(8,128)(2,1)S(1)} %get-tuple-element.4), kind=kOutput, calls=%fused_computation.48 | convolution fusion | flops 3355770880 | bytes 23265280 | tf_op jit(solution)/shard_map/dot_general | solution.py:206
  533.4 30.2 %all_to_all.13 = bf16[32,64,160]{2,1,0:T(8,128)(2,1)S(1)} all-to-all(bf16[32,64,160]{2,1,0:T(8,128)(2,1)S(1)} %bitcast.254), channel_id=1, replica_groups=mesh['fsdp'=32,'tp'=1] {'fsdp'}, dimensions={0} | all-to-all | bytes 1310720 | tf_op jit(solution)/shard_map/all_to_all | solution.py:209
  565.1 2.6 reshape.250
  (172 shorter events, 52.8 us)
Async XLA Ops:
  7.2 34.2 %copy-start = (bf16[16,4,1024]{2,1,0:T(4,128)(2,1)S(1)}, bf16[16,4,1024]{2,1,0:T(4,128)(2,1)}, u32[]{:S(2)}) copy-start(bf16[16,4,1024]{2,1,0:T(4,128)(2,1)} %param.22) | copy-start | bytes 393220
  7.2 513.3 %all-gather.2.cloned.1.call-start = ((), (), s32[]{:S(2)}) async-start(), calls=%async_computation.1 | async-start | bytes 21626880 | tf_op jit(solution)/shard_map/all_gather | solution.py:205
  7.2 111.1 %collective-permute-start = (bf16[1024,5120]{1,0:T(8,128)(2,1)}, bf16[1024,5120]{1,0:T(8,128)(2,1)}, u32[]{:S(2)}, u32[]{:S(2)}) collective-permute-start(bf16[1024,5120]{1,0:T(8,128)(2,1)} %param.14), channel_id=1, source_target_pairs={{0,1},{1,0},{2,3},{3,2},{4,5},{5,4},{6,7},{7,6},{8,9},{9,8},{10,11... | collective-permute-start | bytes 31457288 | tf_op jit(solution)/shard_map/ppermute | solution.py:180
  10.4 11.2 %copy-start.13 = (bf16[16,4,1024]{2,1,0:T(4,128)(2,1)S(1)}, bf16[16,4,1024]{2,1,0:T(4,128)(2,1)}, u32[]{:S(2)}) copy-start(bf16[16,4,1024]{2,1,0:T(4,128)(2,1)} %param.21) | copy-start | bytes 393220
  21.7 11.4 %slice-start = ((s8[8388608]{0:T(1024)(128)(4,1)}), s8[4194304]{0:T(1024)(128)(4,1)S(1)}, s32[]{:S(2)}) async-start(s8[8388608]{0:T(1024)(128)(4,1)} %bitcast.241), calls=%async_computation.2 | async-start | bytes 8388608
  26.5 6.6 %slice-start.1 = ((s8[8388608]{0:T(1024)(128)(4,1)}), s8[4194304]{0:T(1024)(128)(4,1)S(1)}, s32[]{:S(2)}) async-start(s8[8388608]{0:T(1024)(128)(4,1)} %bitcast.241), calls=%async_computation.3 | async-start | bytes 8388608
  44.1 9.0 %copy-start.14 = (f32[2]{0:T(128)S(1)}, f32[2]{0:T(128)}, u32[]{:S(2)}) copy-start(f32[2]{0:T(128)} %param.15) | copy-start | bytes 28
  44.1 53.8 %copy-start.15 = (s32[64]{0:T(128)S(1)}, s32[64]{0:T(128)}, u32[]{:S(2)}) copy-start(s32[64]{0:T(128)} %param.16) | copy-start | bytes 772
  53.1 54.4 %collective-permute-start.1 = (bf16[1024,2560]{1,0:T(8,128)(2,1)}, bf16[1024,2560]{1,0:T(8,128)(2,1)}, u32[]{:S(2)}, u32[]{:S(2)}) collective-permute-start(bf16[1024,2560]{1,0:T(8,128)(2,1)} %get-tuple-element.10), channel_id=1, source_target_pairs={{0,1},{1,0},{2,3},{3,2},{4,5},{5,4},{6,7},{7,6},{8,9},{9,8},{10,11... | collective-permute-start | bytes 15728648 | tf_op jit(solution)/shard_map/ppermute | solution.py:181
  146.0 91.4 %collective-permute-start.2 = (bf16[4,2,320,256]{3,2,0,1:T(8,128)(2,1)}, bf16[4,2,320,256]{3,2,0,1:T(8,128)(2,1)}, u32[]{:S(2)}, u32[]{:S(2)}) collective-permute-start(bf16[4,2,320,256]{3,2,0,1:T(8,128)(2,1)} %select_bitcast_fusion.9), channel_id=1, source_target_pairs={{0,2},{1,3},{2,0},{3,1},{4,6},{5,7},{6,4},{7,5},{8,10},{9,11},{10,... | collective-permute-start | bytes 3932168 | tf_op jit(solution)/shard_map/ppermute | solution.py:88
  150.0 91.1 %collective-permute-start.4 = (bf16[4,2,320,256]{3,2,1,0:T(8,128)(2,1)}, bf16[4,2,320,256]{3,2,1,0:T(8,128)(2,1)}, u32[]{:S(2)}, u32[]{:S(2)}) collective-permute-start(bf16[4,2,320,256]{3,2,1,0:T(8,128)(2,1)} %get-tuple-element.27), channel_id=1, source_target_pairs={{0,4},{1,5},{2,6},{3,7},{4,0},{5,1},{6,2},{7,3},{8,12},{9,13},{10,... | collective-permute-start | bytes 3932168 | tf_op jit(solution)/shard_map/ppermute | solution.py:88
  169.1 75.1 %collective-permute-start.9 = (bf16[4,2,320,256]{3,2,0,1:T(8,128)(2,1)}, bf16[4,2,320,256]{3,2,0,1:T(8,128)(2,1)}, u32[]{:S(2)}, u32[]{:S(2)}) collective-permute-start(bf16[4,2,320,256]{3,2,0,1:T(8,128)(2,1)} %select_bitcast_fusion.7), channel_id=1, source_target_pairs={{0,2},{1,3},{2,0},{3,1},{4,6},{5,7},{6,4},{7,5},{8,10},{9,11},{10,... | collective-permute-start | bytes 3932168 | tf_op jit(solution)/shard_map/ppermute | solution.py:88
  171.1 76.1 %collective-permute-start.11 = (bf16[4,2,320,256]{3,2,0,1:T(8,128)(2,1)}, bf16[4,2,320,256]{3,2,0,1:T(8,128)(2,1)}, u32[]{:S(2)}, u32[]{:S(2)}) collective-permute-start(bf16[4,2,320,256]{3,2,0,1:T(8,128)(2,1)} %select_bitcast_fusion.6), channel_id=1, source_target_pairs={{0,4},{1,5},{2,6},{3,7},{4,0},{5,1},{6,2},{7,3},{8,12},{9,13},{10,... | collective-permute-start | bytes 3932168 | tf_op jit(solution)/shard_map/ppermute | solution.py:88
  189.0 5.2 copy-start.4
  192.3 57.8 %collective-permute-start.16 = (bf16[4,2,320,256]{3,2,0,1:T(8,128)(2,1)}, bf16[4,2,320,256]{3,2,0,1:T(8,128)(2,1)}, u32[]{:S(2)}, u32[]{:S(2)}) collective-permute-start(bf16[4,2,320,256]{3,2,0,1:T(8,128)(2,1)} %select_bitcast_fusion.5), channel_id=1, source_target_pairs={{0,2},{1,3},{2,0},{3,1},{4,6},{5,7},{6,4},{7,5},{8,10},{9,11},{10,... | collective-permute-start | bytes 3932168 | tf_op jit(solution)/shard_map/ppermute | solution.py:88
  237.5 31.8 %collective-permute-start.18 = (bf16[4,2,320,256]{3,2,0,1:T(8,128)(2,1)S(1)}, bf16[4,2,320,256]{3,2,0,1:T(8,128)(2,1)S(1)}, u32[]{:S(2)}, u32[]{:S(2)}) collective-permute-start(bf16[4,2,320,256]{3,2,0,1:T(8,128)(2,1)S(1)} %select_bitcast_fusion.4), channel_id=1, source_target_pairs={{0,4},{1,5},{2,6},{3,7},{4,0},{5,1},{6,2},{7,3},{8,12},{9,13},{10,... | collective-permute-start | bytes 3932168 | tf_op jit(solution)/shard_map/ppermute | solution.py:88
  241.1 31.8 %collective-permute-start.23 = (bf16[4,2,320,256]{3,2,0,1:T(8,128)(2,1)S(1)}, bf16[4,2,320,256]{3,2,0,1:T(8,128)(2,1)S(1)}, u32[]{:S(2)}, u32[]{:S(2)}) collective-permute-start(bf16[4,2,320,256]{3,2,0,1:T(8,128)(2,1)S(1)} %select_bitcast_fusion.3), channel_id=1, source_target_pairs={{0,2},{1,3},{2,0},{3,1},{4,6},{5,7},{6,4},{7,5},{8,10},{9,11},{10,... | collective-permute-start | bytes 3932168 | tf_op jit(solution)/shard_map/ppermute | solution.py:88
  244.2 53.1 %collective-permute-start.25 = (bf16[4,2,320,256]{3,2,0,1:T(8,128)(2,1)S(1)}, bf16[4,2,320,256]{3,2,0,1:T(8,128)(2,1)S(1)}, u32[]{:S(2)}, u32[]{:S(2)}) collective-permute-start(bf16[4,2,320,256]{3,2,0,1:T(8,128)(2,1)S(1)} %select_bitcast_fusion.2), channel_id=1, source_target_pairs={{0,4},{1,5},{2,6},{3,7},{4,0},{5,1},{6,2},{7,3},{8,12},{9,13},{10,... | collective-permute-start | bytes 3932168 | tf_op jit(solution)/shard_map/ppermute | solution.py:88
  247.3 53.7 %collective-permute-start.30 = (bf16[4,2,320,256]{3,2,0,1:T(8,128)(2,1)S(1)}, bf16[4,2,320,256]{3,2,0,1:T(8,128)(2,1)S(1)}, u32[]{:S(2)}, u32[]{:S(2)}) collective-permute-start(bf16[4,2,320,256]{3,2,0,1:T(8,128)(2,1)S(1)} %select_bitcast_fusion.1), channel_id=1, source_target_pairs={{0,2},{1,3},{2,0},{3,1},{4,6},{5,7},{6,4},{7,5},{8,10},{9,11},{10,... | collective-permute-start | bytes 3932168 | tf_op jit(solution)/shard_map/ppermute | solution.py:88
  250.1 75.3 %collective-permute-start.32 = (bf16[4,2,320,256]{3,2,0,1:T(8,128)(2,1)S(1)}, bf16[4,2,320,256]{3,2,0,1:T(8,128)(2,1)S(1)}, u32[]{:S(2)}, u32[]{:S(2)}) collective-permute-start(bf16[4,2,320,256]{3,2,0,1:T(8,128)(2,1)S(1)} %select_bitcast_fusion), channel_id=1, source_target_pairs={{0,4},{1,5},{2,6},{3,7},{4,0},{5,1},{6,2},{7,3},{8,12},{9,13},{10,... | collective-permute-start | bytes 3932168 | tf_op jit(solution)/shard_map/ppermute | solution.py:88
  269.3 70.2 %collective-permute-start.3 = (bf16[4,320,256]{2,1,0:T(8,128)(2,1)S(1)}, bf16[4,320,256]{2,1,0:T(8,128)(2,1)S(1)}, u32[]{:S(2)}, u32[]{:S(2)}) collective-permute-start(bf16[4,320,256]{2,1,0:T(8,128)(2,1)S(1)} %select_bitcast_fusion.18), channel_id=1, source_target_pairs={{0,4},{1,5},{2,6},{3,7},{4,0},{5,1},{6,2},{7,3},{8,12},{9,13},{10,... | collective-permute-start | bytes 1966088 | tf_op jit(solution)/shard_map/ppermute | solution.py:88
  272.8 67.2 %collective-permute-start.5 = (bf16[4,320,256]{2,1,0:T(8,128)(2,1)S(1)}, bf16[4,320,256]{2,1,0:T(8,128)(2,1)S(1)}, u32[]{:S(2)}, u32[]{:S(2)}) collective-permute-start(bf16[4,320,256]{2,1,0:T(8,128)(2,1)S(1)} %fusion.45), channel_id=1, source_target_pairs={{0,2},{1,3},{2,0},{3,1},{4,6},{5,7},{6,4},{7,5},{8,10},{9,11},{10,... | collective-permute-start | bytes 1966088 | tf_op jit(solution)/shard_map/ppermute | solution.py:88
  297.3 56.2 %collective-permute-start.10 = (bf16[4,320,256]{2,1,0:T(8,128)(2,1)S(1)}, bf16[4,320,256]{2,1,0:T(8,128)(2,1)S(1)}, u32[]{:S(2)}, u32[]{:S(2)}) collective-permute-start(bf16[4,320,256]{2,1,0:T(8,128)(2,1)S(1)} %select_bitcast_fusion.17), channel_id=1, source_target_pairs={{0,4},{1,5},{2,6},{3,7},{4,0},{5,1},{6,2},{7,3},{8,12},{9,13},{10,... | collective-permute-start | bytes 1966088 | tf_op jit(solution)/shard_map/ppermute | solution.py:88
  300.9 53.2 %collective-permute-start.12 = (bf16[4,320,256]{2,1,0:T(8,128)(2,1)S(1)}, bf16[4,320,256]{2,1,0:T(8,128)(2,1)S(1)}, u32[]{:S(2)}, u32[]{:S(2)}) collective-permute-start(bf16[4,320,256]{2,1,0:T(8,128)(2,1)S(1)} %select_bitcast_fusion.16), channel_id=1, source_target_pairs={{0,2},{1,3},{2,0},{3,1},{4,6},{5,7},{6,4},{7,5},{8,10},{9,11},{10,... | collective-permute-start | bytes 1966088 | tf_op jit(solution)/shard_map/ppermute | solution.py:88
  325.4 42.1 %collective-permute-start.17 = (bf16[4,320,256]{2,1,0:T(8,128)(2,1)S(1)}, bf16[4,320,256]{2,1,0:T(8,128)(2,1)S(1)}, u32[]{:S(2)}, u32[]{:S(2)}) collective-permute-start(bf16[4,320,256]{2,1,0:T(8,128)(2,1)S(1)} %select_bitcast_fusion.15), channel_id=1, source_target_pairs={{0,4},{1,5},{2,6},{3,7},{4,0},{5,1},{6,2},{7,3},{8,12},{9,13},{10,... | collective-permute-start | bytes 1966088 | tf_op jit(solution)/shard_map/ppermute | solution.py:88
  339.5 28.7 %collective-permute-start.19 = (bf16[4,320,256]{2,1,0:T(8,128)(2,1)S(1)}, bf16[4,320,256]{2,1,0:T(8,128)(2,1)S(1)}, u32[]{:S(2)}, u32[]{:S(2)}) collective-permute-start(bf16[4,320,256]{2,1,0:T(8,128)(2,1)S(1)} %select_bitcast_fusion.14), channel_id=1, source_target_pairs={{0,2},{1,3},{2,0},{3,1},{4,6},{5,7},{6,4},{7,5},{8,10},{9,11},{10,... | collective-permute-start | bytes 1966088 | tf_op jit(solution)/shard_map/ppermute | solution.py:88
  340.1 41.6 %collective-permute-start.24 = (bf16[4,320,256]{2,1,0:T(8,128)(2,1)S(1)}, bf16[4,320,256]{2,1,0:T(8,128)(2,1)S(1)}, u32[]{:S(2)}, u32[]{:S(2)}) collective-permute-start(bf16[4,320,256]{2,1,0:T(8,128)(2,1)S(1)} %select_bitcast_fusion.13), channel_id=1, source_target_pairs={{0,4},{1,5},{2,6},{3,7},{4,0},{5,1},{6,2},{7,3},{8,12},{9,13},{10,... | collective-permute-start | bytes 1966088 | tf_op jit(solution)/shard_map/ppermute | solution.py:88
  353.5 30.6 %collective-permute-start.26 = (bf16[4,320,256]{2,1,0:T(8,128)(2,1)S(1)}, bf16[4,320,256]{2,1,0:T(8,128)(2,1)S(1)}, u32[]{:S(2)}, u32[]{:S(2)}) collective-permute-start(bf16[4,320,256]{2,1,0:T(8,128)(2,1)S(1)} %select_bitcast_fusion.12), channel_id=1, source_target_pairs={{0,2},{1,3},{2,0},{3,1},{4,6},{5,7},{6,4},{7,5},{8,10},{9,11},{10,... | collective-permute-start | bytes 1966088 | tf_op jit(solution)/shard_map/ppermute | solution.py:88
  354.1 38.3 %collective-permute-start.31 = (bf16[4,320,256]{2,1,0:T(8,128)(2,1)S(1)}, bf16[4,320,256]{2,1,0:T(8,128)(2,1)S(1)}, u32[]{:S(2)}, u32[]{:S(2)}) collective-permute-start(bf16[4,320,256]{2,1,0:T(8,128)(2,1)S(1)} %select_bitcast_fusion.11), channel_id=1, source_target_pairs={{0,4},{1,5},{2,6},{3,7},{4,0},{5,1},{6,2},{7,3},{8,12},{9,13},{10,... | collective-permute-start | bytes 1966088 | tf_op jit(solution)/shard_map/ppermute | solution.py:88
  367.6 27.9 %collective-permute-start.33 = (bf16[4,320,256]{2,1,0:T(8,128)(2,1)S(1)}, bf16[4,320,256]{2,1,0:T(8,128)(2,1)S(1)}, u32[]{:S(2)}, u32[]{:S(2)}) collective-permute-start(bf16[4,320,256]{2,1,0:T(8,128)(2,1)S(1)} %select_bitcast_fusion.10), channel_id=1, source_target_pairs={{0,2},{1,3},{2,0},{3,1},{4,6},{5,7},{6,4},{7,5},{8,10},{9,11},{10,... | collective-permute-start | bytes 1966088 | tf_op jit(solution)/shard_map/ppermute | solution.py:88
  368.1 28.3 %collective-permute-start.8 = (bf16[320,512]{1,0:T(8,128)(2,1)S(1)}, bf16[320,512]{1,0:T(8,128)(2,1)S(1)}, u32[]{:S(2)}, u32[]{:S(2)}) collective-permute-start(bf16[320,512]{1,0:T(8,128)(2,1)S(1)} %get-tuple-element.48), channel_id=1, source_target_pairs={{0,24},{1,25},{2,26},{3,27},{4,28},{5,29},{6,30},{7,31},{8,0},{9,1... | collective-permute-start | bytes 983048 | tf_op jit(solution)/shard_map/ppermute | solution.py:128
  381.6 31.1 %collective-permute-start.7 = (bf16[320,512]{1,0:T(8,128)(2,1)S(1)}, bf16[320,512]{1,0:T(8,128)(2,1)S(1)}, u32[]{:S(2)}, u32[]{:S(2)}) collective-permute-start(bf16[320,512]{1,0:T(8,128)(2,1)S(1)} %get-tuple-element.47), channel_id=1, source_target_pairs={{0,16},{1,17},{2,18},{3,19},{4,20},{5,21},{6,22},{7,23},{8,24},{9,... | collective-permute-start | bytes 983048 | tf_op jit(solution)/shard_map/ppermute | solution.py:128
  384.2 28.6 %collective-permute-start.6 = (bf16[320,512]{1,0:T(8,128)(2,1)S(1)}, bf16[320,512]{1,0:T(8,128)(2,1)S(1)}, u32[]{:S(2)}, u32[]{:S(2)}) collective-permute-start(bf16[320,512]{1,0:T(8,128)(2,1)S(1)} %get-tuple-element.46), channel_id=1, source_target_pairs={{0,8},{1,9},{2,10},{3,11},{4,12},{5,13},{6,14},{7,15},{8,16},{9,17... | collective-permute-start | bytes 983048 | tf_op jit(solution)/shard_map/ppermute | solution.py:128
  392.4 38.0 %collective-permute-start.15 = (bf16[320,512]{1,0:T(8,128)(2,1)S(1)}, bf16[320,512]{1,0:T(8,128)(2,1)S(1)}, u32[]{:S(2)}, u32[]{:S(2)}) collective-permute-start(bf16[320,512]{1,0:T(8,128)(2,1)S(1)} %get-tuple-element.45), channel_id=1, source_target_pairs={{0,24},{1,25},{2,26},{3,27},{4,28},{5,29},{6,30},{7,31},{8,0},{9,1... | collective-permute-start | bytes 983048 | tf_op jit(solution)/shard_map/ppermute | solution.py:128
  395.5 48.2 %collective-permute-start.14 = (bf16[320,512]{1,0:T(8,128)(2,1)S(1)}, bf16[320,512]{1,0:T(8,128)(2,1)S(1)}, u32[]{:S(2)}, u32[]{:S(2)}) collective-permute-start(bf16[320,512]{1,0:T(8,128)(2,1)S(1)} %get-tuple-element.44), channel_id=1, source_target_pairs={{0,16},{1,17},{2,18},{3,19},{4,20},{5,21},{6,22},{7,23},{8,24},{9,... | collective-permute-start | bytes 983048 | tf_op jit(solution)/shard_map/ppermute | solution.py:128
  396.4 47.4 %collective-permute-start.13 = (bf16[320,512]{1,0:T(8,128)(2,1)S(1)}, bf16[320,512]{1,0:T(8,128)(2,1)S(1)}, u32[]{:S(2)}, u32[]{:S(2)}) collective-permute-start(bf16[320,512]{1,0:T(8,128)(2,1)S(1)} %get-tuple-element.43), channel_id=1, source_target_pairs={{0,8},{1,9},{2,10},{3,11},{4,12},{5,13},{6,14},{7,15},{8,16},{9,17... | collective-permute-start | bytes 983048 | tf_op jit(solution)/shard_map/ppermute | solution.py:128
  412.7 45.7 %collective-permute-start.22 = (bf16[320,512]{1,0:T(8,128)(2,1)S(1)}, bf16[320,512]{1,0:T(8,128)(2,1)S(1)}, u32[]{:S(2)}, u32[]{:S(2)}) collective-permute-start(bf16[320,512]{1,0:T(8,128)(2,1)S(1)} %get-tuple-element.42), channel_id=1, source_target_pairs={{0,24},{1,25},{2,26},{3,27},{4,28},{5,29},{6,30},{7,31},{8,0},{9,1... | collective-permute-start | bytes 983048 | tf_op jit(solution)/shard_map/ppermute | solution.py:128
  412.8 58.9 %collective-permute-start.21 = (bf16[320,512]{1,0:T(8,128)(2,1)S(1)}, bf16[320,512]{1,0:T(8,128)(2,1)S(1)}, u32[]{:S(2)}, u32[]{:S(2)}) collective-permute-start(bf16[320,512]{1,0:T(8,128)(2,1)S(1)} %get-tuple-element.41), channel_id=1, source_target_pairs={{0,16},{1,17},{2,18},{3,19},{4,20},{5,21},{6,22},{7,23},{8,24},{9,... | collective-permute-start | bytes 983048 | tf_op jit(solution)/shard_map/ppermute | solution.py:128
  430.4 41.4 %collective-permute-start.20 = (bf16[320,512]{1,0:T(8,128)(2,1)S(1)}, bf16[320,512]{1,0:T(8,128)(2,1)S(1)}, u32[]{:S(2)}, u32[]{:S(2)}) collective-permute-start(bf16[320,512]{1,0:T(8,128)(2,1)S(1)} %get-tuple-element.40), channel_id=1, source_target_pairs={{0,8},{1,9},{2,10},{3,11},{4,12},{5,13},{6,14},{7,15},{8,16},{9,17... | collective-permute-start | bytes 983048 | tf_op jit(solution)/shard_map/ppermute | solution.py:128
  443.7 42.9 %collective-permute-start.29 = (bf16[320,512]{1,0:T(8,128)(2,1)S(1)}, bf16[320,512]{1,0:T(8,128)(2,1)S(1)}, u32[]{:S(2)}, u32[]{:S(2)}) collective-permute-start(bf16[320,512]{1,0:T(8,128)(2,1)S(1)} %get-tuple-element.39), channel_id=1, source_target_pairs={{0,24},{1,25},{2,26},{3,27},{4,28},{5,29},{6,30},{7,31},{8,0},{9,1... | collective-permute-start | bytes 983048 | tf_op jit(solution)/shard_map/ppermute | solution.py:128
  443.9 56.0 %collective-permute-start.28 = (bf16[320,512]{1,0:T(8,128)(2,1)S(1)}, bf16[320,512]{1,0:T(8,128)(2,1)S(1)}, u32[]{:S(2)}, u32[]{:S(2)}) collective-permute-start(bf16[320,512]{1,0:T(8,128)(2,1)S(1)} %get-tuple-element.38), channel_id=1, source_target_pairs={{0,16},{1,17},{2,18},{3,19},{4,20},{5,21},{6,22},{7,23},{8,24},{9,... | collective-permute-start | bytes 983048 | tf_op jit(solution)/shard_map/ppermute | solution.py:128
  458.5 41.4 %collective-permute-start.27 = (bf16[320,512]{1,0:T(8,128)(2,1)S(1)}, bf16[320,512]{1,0:T(8,128)(2,1)S(1)}, u32[]{:S(2)}, u32[]{:S(2)}) collective-permute-start(bf16[320,512]{1,0:T(8,128)(2,1)S(1)} %get-tuple-element.37), channel_id=1, source_target_pairs={{0,8},{1,9},{2,10},{3,11},{4,12},{5,13},{6,14},{7,15},{8,16},{9,17... | collective-permute-start | bytes 983048 | tf_op jit(solution)/shard_map/ppermute | solution.py:128
  471.8 28.3 %collective-permute-start.36 = (bf16[320,512]{1,0:T(8,128)(2,1)S(1)}, bf16[320,512]{1,0:T(8,128)(2,1)S(1)}, u32[]{:S(2)}, u32[]{:S(2)}) collective-permute-start(bf16[320,512]{1,0:T(8,128)(2,1)S(1)} %get-tuple-element.36), channel_id=1, source_target_pairs={{0,24},{1,25},{2,26},{3,27},{4,28},{5,29},{6,30},{7,31},{8,0},{9,1... | collective-permute-start | bytes 983048 | tf_op jit(solution)/shard_map/ppermute | solution.py:128
  471.8 40.4 %collective-permute-start.35 = (bf16[320,512]{1,0:T(8,128)(2,1)S(1)}, bf16[320,512]{1,0:T(8,128)(2,1)S(1)}, u32[]{:S(2)}, u32[]{:S(2)}) collective-permute-start(bf16[320,512]{1,0:T(8,128)(2,1)S(1)} %get-tuple-element.35), channel_id=1, source_target_pairs={{0,16},{1,17},{2,18},{3,19},{4,20},{5,21},{6,22},{7,23},{8,24},{9,... | collective-permute-start | bytes 983048 | tf_op jit(solution)/shard_map/ppermute | solution.py:128
  486.6 25.6 %collective-permute-start.34 = (bf16[320,512]{1,0:T(8,128)(2,1)S(1)}, bf16[320,512]{1,0:T(8,128)(2,1)S(1)}, u32[]{:S(2)}, u32[]{:S(2)}) collective-permute-start(bf16[320,512]{1,0:T(8,128)(2,1)S(1)} %get-tuple-element.34), channel_id=1, source_target_pairs={{0,8},{1,9},{2,10},{3,11},{4,12},{5,13},{6,14},{7,15},{8,16},{9,17... | collective-permute-start | bytes 983048 | tf_op jit(solution)/shard_map/ppermute | solution.py:128
  512.2 4.0 copy-start.11
  512.6 3.6 collective-permute-start.37
  563.8 3.9 copy-start.1
  (9 other events, 22.4 us)
Sparse Core Ops, SparseCore 0:
  44.2 144.6 all-gather.1
